TPU v7x, 768 devices: a whole 4x8x12 slice. The times are simulated.
768 devices in a mesh: row: 24 (over z, y_hi), col: 32 (over y_lo, x, core).
Axes of the slice: x: 4, y: 8 (y_hi: 2, y_lo: 4; y = y_hi * 4 + y_lo), z: 12, core: 2. Of those that a mesh axis runs over, the one named last changes fastest.
Arguments:
- vectors: float32 [786432, 256], P(('row', 'col')), may hold values from -6 to 6
- blocks: float32 [6144, 5, 128, 128], P(('row', 'col')), may hold values from -0.25 to 0.25
- pattern: int32 [6144, 5], P(('row', 'col')), may hold values from 0 to 6143, as said below
- counts: int32 [6144], P(('row', 'col')), may hold values from 1 to 5, as said below
Outputs:
- filtered: float32 [786432, 256], P(('row', 'col'))
Inputs may be any that keep to these rules, and one draw needn't show every extreme that they name: `pattern`: block row a = ((r * 32 + c) * 2 + u) * 4 + v is the site (r * 2 + u, c * 4 + v) of a periodic lattice of 48 x 128 sites; its 5 slots name, in an order that varies from row to row, the block rows of that site and of the four sites one step away along either lattice direction, with wrap-around. The live slots of a block row are its first counts ones; some block row holds exactly 5 live slots and some exactly 1.
All inputs are finite; a program needn't handle non-finite values.
Results may differ from a plain program's by a relative error of at most 0.000084.
Values sent between devices are 32-bit elements; how exact they have to be, the bound alone decides.
A program may use at most 64 MiB of HBM per device.

v0:
```python
import jax
import jax.numpy as jnp
from jax import lax
from jax.sharding import PartitionSpec as P

TY = 2


center_shift = 0.25
half_range = 1.0


def padded(block, sides, width):
    for axis, dim in sides:
        count = lax.axis_size(axis)
        forward = [(i, i + 1) for i in range(count - 1)]
        forward.append((count - 1, 0))
        backward = [(target, source) for source, target in forward]
        low = lax.ppermute(
            lax.slice_in_dim(block, block.shape[dim] - width, None, axis=dim), axis, forward
        )
        high = lax.ppermute(lax.slice_in_dim(block, 0, width, axis=dim), axis, backward)
        block = jnp.concatenate([low, block, high], axis=dim)
    return block


def body(vectors, blocks, pattern, counts):
    local_blocks = blocks.shape[0]
    slot_total = blocks.shape[1]
    block_size = blocks.shape[-1]
    width = vectors.shape[1]
    row_count = lax.axis_size("row")
    col_count = lax.axis_size("col")
    lat_cols = local_blocks // TY
    span_y = TY * row_count
    span_x = lat_cols * col_count
    local_ids = jnp.arange(local_blocks, dtype=jnp.int32)
    here_y = local_ids // lat_cols
    here_x = local_ids % lat_cols
    own_y = lax.axis_index("row") * TY + here_y
    own_x = lax.axis_index("col") * lat_cols + here_x
    target_owner = pattern // (lat_cols * TY)
    target_y = target_owner // col_count * TY + pattern // lat_cols % TY
    target_x = target_owner % col_count * lat_cols + pattern % lat_cols
    step_y = jnp.remainder(target_y - own_y[:, None] + 1, span_y) - 1
    step_x = jnp.remainder(target_x - own_x[:, None] + 1, span_x) - 1
    place = (here_y[:, None] + 1 + step_y) * (lat_cols + 2) + here_x[:, None] + 1 + step_x
    live = (jnp.arange(slot_total, dtype=jnp.int32)[None, :] < counts[:, None]).astype(jnp.float32)
    masked_blocks = blocks * live[:, :, None, None]

    def build_canvas(field):
        grid = field.reshape(TY, lat_cols, block_size, width)
        tall = padded(grid, (("row", 0),), 1)
        broad = padded(grid, (("col", 1),), 1)
        canvas = jnp.zeros((TY + 2, lat_cols + 2, block_size, width), jnp.float32)
        canvas = canvas.at[:, 1:-1].set(tall)
        canvas = canvas.at[1:-1, :].set(broad)
        return canvas.reshape(-1, block_size, width)

    def apply_hamiltonian(field):
        pool = build_canvas(field)
        columns = pool[place]
        total = jnp.einsum(
            "bsij,bsjw->biw",
            masked_blocks,
            columns,
            precision=lax.Precision.HIGHEST,
            preferred_element_type=jnp.float32,
        )
        return total.reshape(local_blocks * block_size, width)

    first = (apply_hamiltonian(vectors) - center_shift * vectors) / half_range
    second = apply_hamiltonian(first)
    return 2.0 / half_range * (second - center_shift * first) - vectors


def solution(mesh):
    placed = (
        P(("row", "col"), None),
        P(("row", "col"), None, None, None),
        P(("row", "col"), None),
        P(("row", "col")),
    )
    return jax.shard_map(
        body, mesh=mesh, in_specs=placed, out_specs=P(("row", "col"), None), check_vma=False
    )
```

profile of v0, /device:TPU:721, one launch (start us, length us, event | category | flops | bytes accessed | tf_op | source)
XLA Modules:
  0.0 156.2 jit_solution(8808233706182118179)
XLA Ops:
  0.0 0.0 copy-start
  0.0 0.0 copy-start.1
  0.0 0.0 copy-start.2
  0.0 1.9 %fusion.34 = (f32[2,1,128,256]{3,2,1,0:T(8,128)}, f32[2,1,128,256]{3,2,1,0:T(8,128)}) fusion(f32[2,4,128,256]{3,2,1,0:T(8,128)} %bitcast.28), kind=kLoop, calls=%fused_computation.79 | loop fusion | bytes 1048576 | tf_op jit(solution)/shard_map/slice | solution.py:20
  1.9 3.7 %collective-permute-start.2 = (f32[2,1,128,256]{3,2,1,0:T(8,128)}, f32[2,1,128,256]{3,2,1,0:T(8,128)S(1)}, u32[]{:S(2)}, u32[]{:S(2)}) collective-permute-start(f32[2,1,128,256]{3,2,1,0:T(8,128)} %get-tuple-element.57), channel_id=1, source_target_pairs={{0,1},{1,2},{2,3},{3,4},{4,5},{5,6},{6,7},{7,8},{8,9},{9,10},{10,1... | collective-permute-start | bytes 786440 | tf_op jit(solution)/shard_map/ppermute | solution.py:19
  5.6 1.9 %collective-permute-start.3 = (f32[2,1,128,256]{3,2,1,0:T(8,128)}, f32[2,1,128,256]{3,2,1,0:T(8,128)}, u32[]{:S(2)}, u32[]{:S(2)}) collective-permute-start(f32[2,1,128,256]{3,2,1,0:T(8,128)} %get-tuple-element.58), channel_id=1, source_target_pairs={{1,0},{2,1},{3,2},{4,3},{5,4},{6,5},{7,6},{8,7},{9,8},{10,9},{11,1... | collective-permute-start | bytes 786440 | tf_op jit(solution)/shard_map/ppermute | solution.py:22
  7.6 1.3 fusion.35
  8.8 5.6 %collective-permute-start.1 = (f32[1,4,128,256]{3,2,1,0:T(8,128)S(1)}, f32[1,4,128,256]{3,2,1,0:T(8,128)S(1)}, u32[]{:S(2)}, u32[]{:S(2)}) collective-permute-start(f32[1,4,128,256]{3,2,1,0:T(8,128)S(1)} %bitcast.37), channel_id=1, source_target_pairs={{32,0},{64,32},{96,64},{128,96},{160,128},{192,160},{224,192},{256... | collective-permute-start | bytes 1572872 | tf_op jit(solution)/shard_map/ppermute | solution.py:22
  14.5 3.5 %collective-permute-start = (f32[1,4,128,256]{3,2,1,0:T(8,128)S(1)}, f32[1,4,128,256]{3,2,1,0:T(8,128)S(1)}, u32[]{:S(2)}, u32[]{:S(2)}) collective-permute-start(f32[1,4,128,256]{3,2,1,0:T(8,128)S(1)} %bitcast.36), channel_id=1, source_target_pairs={{0,32},{32,64},{64,96},{96,128},{128,160},{160,192},{192,224},{224... | collective-permute-start | bytes 1572872 | tf_op jit(solution)/shard_map/ppermute | solution.py:19
  18.1 0.0 copy-done.1
  18.1 0.1 compare_select_fusion
  18.2 0.1 reshape.217
  18.3 0.0 copy-done.2
  18.3 0.1 fusion.28
  18.3 49.3 %collective-permute-done.1 = f32[1,4,128,256]{3,2,1,0:T(8,128)S(1)} collective-permute-done((f32[1,4,128,256]{3,2,1,0:T(8,128)S(1)}, f32[1,4,128,256]{3,2,1,0:T(8,128)S(1)}, u32[]{:S(2)}, u32[]{:S(2)}) %collective-permute-start.1) | collective-permute-done | bytes 524320 | tf_op jit(solution)/shard_map/ppermute | solution.py:22
  67.6 0.0 collective-permute-done
  67.6 0.0 copy-done
  67.6 2.0 %select_maximum_fusion.2 = f32[4,6,128,256]{3,2,1,0:T(8,128)} fusion(f32[1,4,128,256]{3,2,1,0:T(8,128)S(1)} %collective-permute-done.1, f32[2,4,128,256]{3,2,1,0:T(8,128)S(1)} %bitcast.29, f32[1,4,128,256]{3,2,1,0:T(8,128)S(1)} %collective-permute-done), kind=kLoop, calls=%fused_computation.6 | loop fusion | flops 6291456 | bytes 5242880 | tf_op jit(solution)/shard_map/concatenate | solution.py:23
  69.6 0.0 collective-permute-done.2
  69.6 0.0 collective-permute-done.3
  69.6 2.2 %maximum_dynamic-update-slice_fusion = f32[4,6,128,256]{3,2,1,0:T(8,128)} fusion(f32[4,6,128,256]{3,2,1,0:T(8,128)} %select_maximum_fusion.2, f32[2,1,128,256]{3,2,1,0:T(8,128)} %collective-permute-done.3, f32[2,4,128,256]{3,2,1,0:T(8,128)S(1)} %bitcast.30, f32[2,1,128,256]{3,2,1,0:T(8,128)S(1)} %collective-permute-done.2), kind=kLoop, calls=%fused_computation.13 | loop fusion | flops 786432 | bytes 3145728 | tf_op jit(solution)/shard_map/scatter | solution.py:57
  71.8 5.1 %gather_fusion = f32[40,128,256]{2,1,0:T(8,128)} fusion(f32[24,128,256]{2,1,0:T(8,128)} %bitcast.3, s32[1024]{0:T(1024)S(1)} %pad_clamp_fusion), kind=kCustom, calls=%fused_computation | custom fusion | bytes 10485920 | tf_op jit(solution)/shard_map/gather | solution.py:62
  76.9 6.8 %fusion.3 = f32[8,128,256,1]{2,1,3,0:T(8,128)S(1)} fusion(f32[8,5,128,256]{3,2,1,0:T(8,128)} %bitcast.35, f32[8,5,128,128]{3,2,1,0:T(8,128)} %param.13, f32[8,5]{1,0:T(8,128)S(1)} %fusion.28), kind=kOutput, calls=%fused_computation.11 | convolution fusion | flops 2013921280 | bytes 8913056 | tf_op jit(solution)/shard_map/bsij,bsjw->biw/dot_general | solution.py:63
  83.7 0.1 bitcast_subtract_fusion.1
  83.9 0.1 fusion.33
  84.0 1.9 %collective-permute-start.5 = (f32[1,4,128,256]{3,2,1,0:T(8,128)S(1)}, f32[1,4,128,256]{3,2,1,0:T(8,128)S(1)}, u32[]{:S(2)}, u32[]{:S(2)}) collective-permute-start(f32[1,4,128,256]{3,2,1,0:T(8,128)S(1)} %bitcast.39), channel_id=1, source_target_pairs={{32,0},{64,32},{96,64},{128,96},{160,128},{192,160},{224,192},{256... | collective-permute-start | bytes 1572872 | tf_op jit(solution)/shard_map/ppermute | solution.py:22
  85.9 7.3 %collective-permute-start.4 = (f32[1,4,128,256]{3,2,1,0:T(8,128)S(1)}, f32[1,4,128,256]{3,2,1,0:T(8,128)S(1)}, u32[]{:S(2)}, u32[]{:S(2)}) collective-permute-start(f32[1,4,128,256]{3,2,1,0:T(8,128)S(1)} %bitcast.38), channel_id=1, source_target_pairs={{0,32},{32,64},{64,96},{96,128},{128,160},{160,192},{192,224},{224... | collective-permute-start | bytes 1572872 | tf_op jit(solution)/shard_map/ppermute | solution.py:19
  93.2 1.9 %collective-permute-start.6 = (f32[2,1,128,256]{3,2,1,0:T(8,128)S(1)}, f32[2,1,128,256]{3,2,1,0:T(8,128)S(1)}, u32[]{:S(2)}, u32[]{:S(2)}) collective-permute-start(f32[2,1,128,256]{3,2,1,0:T(8,128)S(1)} %get-tuple-element.53), channel_id=1, source_target_pairs={{0,1},{1,2},{2,3},{3,4},{4,5},{5,6},{6,7},{7,8},{8,9},{9,10},{10,1... | collective-permute-start | bytes 786440 | tf_op jit(solution)/shard_map/ppermute | solution.py:19
  95.1 3.0 %collective-permute-start.7 = (f32[2,1,128,256]{3,2,1,0:T(8,128)S(1)}, f32[2,1,128,256]{3,2,1,0:T(8,128)S(1)}, u32[]{:S(2)}, u32[]{:S(2)}) collective-permute-start(f32[2,1,128,256]{3,2,1,0:T(8,128)S(1)} %get-tuple-element.54), channel_id=1, source_target_pairs={{1,0},{2,1},{3,2},{4,3},{5,4},{6,5},{7,6},{8,7},{9,8},{10,9},{11,1... | collective-permute-start | bytes 786440 | tf_op jit(solution)/shard_map/ppermute | solution.py:22
  98.2 41.7 %collective-permute-done.5 = f32[1,4,128,256]{3,2,1,0:T(8,128)S(1)} collective-permute-done((f32[1,4,128,256]{3,2,1,0:T(8,128)S(1)}, f32[1,4,128,256]{3,2,1,0:T(8,128)S(1)}, u32[]{:S(2)}, u32[]{:S(2)}) %collective-permute-start.5) | collective-permute-done | bytes 524320 | tf_op jit(solution)/shard_map/ppermute | solution.py:22
  139.9 0.0 collective-permute-done.4
  139.9 2.0 %select_maximum_fusion = f32[4,6,128,256]{3,2,1,0:T(8,128)} fusion(f32[1,4,128,256]{3,2,1,0:T(8,128)S(1)} %collective-permute-done.5, f32[2,4,128,256]{3,2,1,0:T(8,128)S(1)} %bitcast.32, f32[1,4,128,256]{3,2,1,0:T(8,128)S(1)} %collective-permute-done.4), kind=kLoop, calls=%fused_computation.4 | loop fusion | flops 6291456 | bytes 5242880 | tf_op jit(solution)/shard_map/concatenate | solution.py:23
  141.9 0.0 collective-permute-done.6
  141.9 0.0 collective-permute-done.7
  141.9 1.2 maximum_dynamic-update-slice_fusion.1
  143.1 5.1 %gather_fusion.1 = f32[40,128,256]{2,1,0:T(8,128)} fusion(f32[24,128,256]{2,1,0:T(8,128)} %bitcast.11, s32[1024]{0:T(1024)S(1)} %pad_clamp_fusion), kind=kCustom, calls=%fused_computation.1 | custom fusion | bytes 10485920 | tf_op jit(solution)/shard_map/gather | solution.py:62
  148.2 6.8 %fusion.1 = f32[8,128,256,1]{2,1,3,0:T(8,128)S(1)} fusion(f32[8,5,128,256]{3,2,1,0:T(8,128)} %bitcast.34, f32[8,5,128,128]{3,2,1,0:T(8,128)} %param.13, f32[8,5]{1,0:T(8,128)S(1)} %fusion.28), kind=kOutput, calls=%fused_computation.9 | convolution fusion | flops 2013921280 | bytes 8913056 | tf_op jit(solution)/shard_map/bsij,bsjw->biw/dot_general | solution.py:63
  155.1 1.2 fusion.8
  (4 shorter events, 0.1 us)
Async XLA Ops:
  0.0 67.6 %copy-start = (f32[1024,256]{1,0:T(8,128)S(1)}, f32[1024,256]{1,0:T(8,128)}, u32[]{:S(2)}) copy-start(f32[1024,256]{1,0:T(8,128)} %param.12) | copy-start | bytes 3145732
  0.0 18.1 %copy-start.1 = (s32[8,5]{1,0:T(8,128)S(1)}, s32[8,5]{1,0:T(8,128)}, u32[]{:S(2)}) copy-start(s32[8,5]{1,0:T(8,128)} %param.14) | copy-start | bytes 484
  0.0 18.3 %copy-start.2 = (s32[8]{0:T(128)S(1)}, s32[8]{0:T(128)}, u32[]{:S(2)}) copy-start(s32[8]{0:T(128)} %param.15) | copy-start | bytes 100
  1.9 67.7 %collective-permute-start.2 = (f32[2,1,128,256]{3,2,1,0:T(8,128)}, f32[2,1,128,256]{3,2,1,0:T(8,128)S(1)}, u32[]{:S(2)}, u32[]{:S(2)}) collective-permute-start(f32[2,1,128,256]{3,2,1,0:T(8,128)} %get-tuple-element.57), channel_id=1, source_target_pairs={{0,1},{1,2},{2,3},{3,4},{4,5},{5,6},{6,7},{7,8},{8,9},{9,10},{10,1... | collective-permute-start | bytes 786440 | tf_op jit(solution)/shard_map/ppermute | solution.py:19
  5.6 64.0 %collective-permute-start.3 = (f32[2,1,128,256]{3,2,1,0:T(8,128)}, f32[2,1,128,256]{3,2,1,0:T(8,128)}, u32[]{:S(2)}, u32[]{:S(2)}) collective-permute-start(f32[2,1,128,256]{3,2,1,0:T(8,128)} %get-tuple-element.58), channel_id=1, source_target_pairs={{1,0},{2,1},{3,2},{4,3},{5,4},{6,5},{7,6},{8,7},{9,8},{10,9},{11,1... | collective-permute-start | bytes 786440 | tf_op jit(solution)/shard_map/ppermute | solution.py:22
  8.8 58.8 %collective-permute-start.1 = (f32[1,4,128,256]{3,2,1,0:T(8,128)S(1)}, f32[1,4,128,256]{3,2,1,0:T(8,128)S(1)}, u32[]{:S(2)}, u32[]{:S(2)}) collective-permute-start(f32[1,4,128,256]{3,2,1,0:T(8,128)S(1)} %bitcast.37), channel_id=1, source_target_pairs={{32,0},{64,32},{96,64},{128,96},{160,128},{192,160},{224,192},{256... | collective-permute-start | bytes 1572872 | tf_op jit(solution)/shard_map/ppermute | solution.py:22
  14.5 53.2 %collective-permute-start = (f32[1,4,128,256]{3,2,1,0:T(8,128)S(1)}, f32[1,4,128,256]{3,2,1,0:T(8,128)S(1)}, u32[]{:S(2)}, u32[]{:S(2)}) collective-permute-start(f32[1,4,128,256]{3,2,1,0:T(8,128)S(1)} %bitcast.36), channel_id=1, source_target_pairs={{0,32},{32,64},{64,96},{96,128},{128,160},{160,192},{192,224},{224... | collective-permute-start | bytes 1572872 | tf_op jit(solution)/shard_map/ppermute | solution.py:19
  84.0 55.9 %collective-permute-start.5 = (f32[1,4,128,256]{3,2,1,0:T(8,128)S(1)}, f32[1,4,128,256]{3,2,1,0:T(8,128)S(1)}, u32[]{:S(2)}, u32[]{:S(2)}) collective-permute-start(f32[1,4,128,256]{3,2,1,0:T(8,128)S(1)} %bitcast.39), channel_id=1, source_target_pairs={{32,0},{64,32},{96,64},{128,96},{160,128},{192,160},{224,192},{256... | collective-permute-start | bytes 1572872 | tf_op jit(solution)/shard_map/ppermute | solution.py:22
  85.9 54.0 %collective-permute-start.4 = (f32[1,4,128,256]{3,2,1,0:T(8,128)S(1)}, f32[1,4,128,256]{3,2,1,0:T(8,128)S(1)}, u32[]{:S(2)}, u32[]{:S(2)}) collective-permute-start(f32[1,4,128,256]{3,2,1,0:T(8,128)S(1)} %bitcast.38), channel_id=1, source_target_pairs={{0,32},{32,64},{64,96},{96,128},{128,160},{160,192},{192,224},{224... | collective-permute-start | bytes 1572872 | tf_op jit(solution)/shard_map/ppermute | solution.py:19
  93.2 48.7 %collective-permute-start.6 = (f32[2,1,128,256]{3,2,1,0:T(8,128)S(1)}, f32[2,1,128,256]{3,2,1,0:T(8,128)S(1)}, u32[]{:S(2)}, u32[]{:S(2)}) collective-permute-start(f32[2,1,128,256]{3,2,1,0:T(8,128)S(1)} %get-tuple-element.53), channel_id=1, source_target_pairs={{0,1},{1,2},{2,3},{3,4},{4,5},{5,6},{6,7},{7,8},{8,9},{9,10},{10,1... | collective-permute-start | bytes 786440 | tf_op jit(solution)/shard_map/ppermute | solution.py:19
  95.1 46.7 %collective-permute-start.7 = (f32[2,1,128,256]{3,2,1,0:T(8,128)S(1)}, f32[2,1,128,256]{3,2,1,0:T(8,128)S(1)}, u32[]{:S(2)}, u32[]{:S(2)}) collective-permute-start(f32[2,1,128,256]{3,2,1,0:T(8,128)S(1)} %get-tuple-element.54), channel_id=1, source_target_pairs={{1,0},{2,1},{3,2},{4,3},{5,4},{6,5},{7,6},{8,7},{9,8},{10,9},{11,1... | collective-permute-start | bytes 786440 | tf_op jit(solution)/shard_map/ppermute | solution.py:22
where the time goes:
time: 157 us; the launch traced here: 156 us
  waiting for transfers between devices  91 us (58%)
  starting transfers between devices  28.9 us (18%)
  matrix products  13.7 us (9%)
  local copies, waits for them, and re-layouts  13.6 us (9%)
  other arithmetic  8.9 us (6%)
    ppermute x4, waiting for transfers between devices, padded(): lax.ppermute(lax.slice_in_dim(block, 0, width, axis=dim), axis, backward)  91 us
    ppermute x4, starting transfers between devices, padded(): lax.ppermute(lax.slice_in_dim(block, block.shape[dim] - width, None, axis...  16.4 us
    dot_general x2, matrix products, apply_hamiltonian(): jnp.einsum('bsij,bsjw->biw', masked_blocks, columns, precision=lax.Precis...  13.7 us
    ppermute x4, starting transfers between devices, padded(): lax.ppermute(lax.slice_in_dim(block, 0, width, axis=dim), axis, backward)  12.5 us
    gather x2, local copies, waits for them, and re-layouts, apply_hamiltonian(): columns = pool[place]  10.1 us
    concatenate x2, other arithmetic, padded(): block = jnp.concatenate([low, block, high], axis=dim)  3.96 us
    scatter x2, other arithmetic, build_canvas(): canvas = canvas.at[1:-1, :].set(broad)  3.45 us
    slice x4, local copies, waits for them, and re-layouts, padded(): lax.slice_in_dim(block, block.shape[dim] - width, None, axis=dim)  3.32 us
  transfers between devices with their start and end apart: 8, of which 2 were waited for; matrix products, arithmetic and copies ran while one was open for 4% of the time, Pallas kernels for 0%

commit v1 on v0

v1 whole, which is shorter than its diff:
```python
import functools

import jax
import jax.numpy as jnp
from jax import lax
from jax.experimental import pallas as pl
from jax.experimental.pallas import tpu as pltpu
from jax.sharding import PartitionSpec as P

TY = 2
MESH = pl.DeviceIdType.MESH

center_shift = 0.25
half_range = 1.0

OWN, INNER, LEFT, RIGHT, OUTER = range(5)


def dot(a, b):
    return jnp.dot(a, b, precision=lax.Precision.HIGHEST, preferred_element_type=jnp.float32)


def kernel(
    rows, cols, tx,
    vec_hbm, blk_hbm, pattern, counts, out_hbm,
    vec, blk, amat, first, out, halo_row, halo_col,
    load_sem, store_sem, row_send, row_recv, col_send, col_recv,
):
    bs = vec.shape[1]
    slots = blk.shape[1]
    sites = TY * tx
    me_r, me_c = lax.axis_index("row"), lax.axis_index("col")
    row_of = (lax.rem(me_r + rows - 1, rows), lax.rem(me_r + 1, rows))
    col_of = (lax.rem(me_c + cols - 1, cols), lax.rem(me_c + 1, cols))
    row_dev = [(r, me_c) for r in row_of]
    col_dev = [(me_r, c) for c in col_of]

    load_blk = pltpu.make_async_copy(blk_hbm, blk, load_sem.at[0])
    load_vec = pltpu.make_async_copy(vec_hbm, vec, load_sem.at[1])
    load_vec.start()
    load_blk.start()

    barrier = pltpu.get_barrier_semaphore()
    for device in row_dev + col_dev:
        pl.semaphore_signal(barrier, inc=1, device_id=device, device_id_type=MESH)
    pl.semaphore_wait(barrier, 4)

    def row_copy(source, step, u, v):
        return pltpu.make_async_remote_copy(
            src_ref=source.at[u * tx + v], dst_ref=halo_row.at[step, 1 - u, v],
            send_sem=row_send.at[step, 1 - u, v], recv_sem=row_recv.at[step, 1 - u, v],
            device_id=row_dev[u], device_id_type=MESH,
        )

    def col_copy(source, step, side, u):
        v = 0 if side == 0 else tx - 1
        return pltpu.make_async_remote_copy(
            src_ref=source.at[u * tx + v], dst_ref=halo_col.at[step, 1 - side, u],
            send_sem=col_send.at[step, 1 - side, u], recv_sem=col_recv.at[step, 1 - side, u],
            device_id=col_dev[side], device_id_type=MESH,
        )

    edges = [0, tx - 1]
    inside = list(range(1, tx - 1))
    for u in range(TY):
        for side in range(2):
            col_copy(vec_hbm, 0, side, u).start()
    for v in edges + inside:
        for u in range(TY):
            row_copy(vec_hbm, 0, u, v).start()

    def site_id(y, x):
        return ((y // TY * cols + x // tx) * TY + y % TY) * tx + x % tx

    load_blk.wait()
    for u in range(TY):
        for v in range(tx):
            a = u * tx + v
            y, x = me_r * TY + u, me_c * tx + v
            up = lax.rem(y + TY * rows - 1, TY * rows)
            down = lax.rem(y + 1, TY * rows)
            left = lax.rem(x + tx * cols - 1, tx * cols)
            right = lax.rem(x + 1, tx * cols)
            target = [(y, x), (down if u == 0 else up, x), (y, left), (y, right), (up if u == 0 else down, x)]
            for d in range(5):
                name = site_id(*target[d])
                slot = jnp.int32(0)
                for s in range(1, slots):
                    slot = jnp.where(pattern[a, s] == name, s, slot)
                live = jnp.where(slot < counts[a], 1.0, 0.0)
                amat[a, :, d * bs:(d + 1) * bs] = blk[a, slot] * live

    load_vec.wait()

    def partial(field, step, u, v):
        a = u * tx + v
        near = [
            field[a],
            field[(1 - u) * tx + v],
            halo_col[step, 0, u] if v == 0 else field[a - 1],
            halo_col[step, 1, u] if v == tx - 1 else field[a + 1],
        ]
        total = dot(amat[a, :, :2 * bs], jnp.concatenate(near[:2], axis=0))
        total += dot(amat[a, :, 2 * bs:4 * bs], jnp.concatenate(near[2:], axis=0))
        return total - center_shift * near[0]

    def outer(step, u, v):
        return dot(amat[u * tx + v, :, 4 * bs:], halo_row[step, u, v])

    for step, field, result in ((0, vec, first), (1, first, out)):
        for v in inside:
            for u in range(TY):
                result[u * tx + v] = partial(field, step, u, v)
        for u in range(TY):
            for side in range(2):
                col_copy(field, step, side, u).wait_recv()
        for v in edges:
            for u in range(TY):
                result[u * tx + v] = partial(field, step, u, v)
        for v in edges + inside:
            for u in range(TY):
                a = u * tx + v
                row_copy(field, step, 1 - u, v).wait_recv()
                total = (result[a] + outer(step, u, v)) / half_range
                if step == 0:
                    first[a] = total
                    row_copy(first, 1, u, v).start()
                    if v == 0:
                        col_copy(first, 1, 0, u).start()
                    if v == tx - 1:
                        col_copy(first, 1, 1, u).start()
                else:
                    out[a] = 2.0 * total - vec[a]
                    pltpu.make_async_copy(out.at[a], out_hbm.at[a], store_sem.at[a]).start()

    for a in range(sites):
        pltpu.make_async_copy(out.at[a], out_hbm.at[a], store_sem.at[a]).wait()
    for step, field in ((0, vec_hbm), (1, first)):
        for u in range(TY):
            for v in range(tx):
                row_copy(field, step, u, v).wait_send()
            for side in range(2):
                col_copy(field, step, side, u).wait_send()


def body(vectors, blocks, pattern, counts):
    local, slots, bs, _ = blocks.shape
    width = vectors.shape[1]
    rows, cols = lax.axis_size("row"), lax.axis_size("col")
    tx = local // TY
    f32 = jnp.float32
    anywhere = pl.BlockSpec(memory_space=pl.ANY)
    scalars = pl.BlockSpec(memory_space=pltpu.SMEM)
    dma = pltpu.SemaphoreType.DMA
    result = pl.pallas_call(
        functools.partial(kernel, rows, cols, tx),
        out_shape=jax.ShapeDtypeStruct((local, bs, width), f32),
        in_specs=[anywhere, anywhere, scalars, scalars],
        out_specs=anywhere,
        scratch_shapes=[
            pltpu.VMEM((local, bs, width), f32),
            pltpu.VMEM((local, slots, bs, bs), f32),
            pltpu.VMEM((local, bs, slots * bs), f32),
            pltpu.VMEM((local, bs, width), f32),
            pltpu.VMEM((local, bs, width), f32),
            pltpu.VMEM((2, 2, tx, bs, width), f32),
            pltpu.VMEM((2, 2, TY, bs, width), f32),
            dma((2,)),
            dma((local,)),
            dma((2, 2, tx)),
            dma((2, 2, tx)),
            dma((2, 2, TY)),
            dma((2, 2, TY)),
        ],
        compiler_params=pltpu.CompilerParams(
            collective_id=0, has_side_effects=True, vmem_limit_bytes=32 << 20
        ),
        cost_estimate=pl.CostEstimate(
            flops=2 * 2 * local * slots * bs * bs * width, bytes_accessed=5 << 20, transcendentals=0
        ),
        name="filter_steps",
    )(vectors.reshape(local, bs, width), blocks, pattern, counts)
    return result.reshape(local * bs, width)


def solution(mesh):
    placed = (
        P(("row", "col"), None),
        P(("row", "col"), None, None, None),
        P(("row", "col"), None),
        P(("row", "col")),
    )
    return jax.shard_map(
        body, mesh=mesh, in_specs=placed, out_specs=P(("row", "col"), None), check_vma=False
    )
```

time: 157 us -> 121 us (0.77)
  the two profiles are of different devices: /device:TPU:721 before, /device:TPU:576 now
where the time goes in v1:
time: 121 us
  Pallas kernels  115 us (95%)
  local copies, waits for them, and re-layouts  5.28 us (4%)
    pallas_call x1, Pallas kernels, body(): pl.pallas_call(functools.partial(kernel, rows, cols, tx), out_shape=jax.S...  115 us
    unnamed x9, local copies, waits for them, and re-layouts  5.28 us

profile of v1, /device:TPU:576, one launch (start us, length us, event | category | flops | bytes accessed | tf_op | source)
XLA Modules:
  0.0 120.6 jit_solution(9002388729760174457)
XLA Ops:
  0.0 0.0 copy-start
  0.0 1.7 %copy-done = f32[8,5,128,128]{3,2,1,0:T(8,128)S(1)} copy-done((f32[8,5,128,128]{3,2,1,0:T(8,128)S(1)}, f32[8,5,128,128]{3,2,1,0:T(8,128)}, u32[]{:S(2)}) %copy-start) | copy-done | bytes 2621464
  1.7 0.0 copy-start.1
  1.7 1.2 %copy-done.1 = f32[1024,256]{1,0:T(8,128)S(1)} copy-done((f32[1024,256]{1,0:T(8,128)S(1)}, f32[1024,256]{1,0:T(8,128)}, u32[]{:S(2)}) %copy-start.1) | copy-done | bytes 1048600
  3.0 0.0 copy-start.2
  3.0 0.7 copy-done.2
  3.7 0.0 copy-start.3
  3.7 0.7 copy-done.3
  4.3 115.3 %filter_steps.1 = f32[8,128,256]{2,1,0:T(8,128)S(1)} custom-call(f32[8,128,256]{2,1,0:T(8,128)S(1)} %bitcast.3, f32[8,5,128,128]{3,2,1,0:T(8,128)S(1)} %copy-done, s32[8,5]{1,0:T(8,128)S(1)} %copy-done.2, s32[8]{0:T(128)S(1)} %copy-done.3), custom_call_target="tpu_custom_call" | custom-call | flops 671088640 | bytes 5242880 | tf_op jit(solution)/shard_map/filter_steps/pallas_call | solution.py:155
  119.6 1.0 copy.6
Async XLA Ops:
  0.0 1.7 %copy-start = (f32[8,5,128,128]{3,2,1,0:T(8,128)S(1)}, f32[8,5,128,128]{3,2,1,0:T(8,128)}, u32[]{:S(2)}) copy-start(f32[8,5,128,128]{3,2,1,0:T(8,128)} %blk_hbm.1) | copy-start | bytes 7864324
  1.7 1.2 %copy-start.1 = (f32[1024,256]{1,0:T(8,128)S(1)}, f32[1024,256]{1,0:T(8,128)}, u32[]{:S(2)}) copy-start(f32[1024,256]{1,0:T(8,128)} %param.4) | copy-start | bytes 3145732
  3.0 0.7 copy-start.2
  3.7 0.7 copy-start.3

commit v2 on v1

v2 whole, which is shorter than its diff:
```python
import functools

import jax
import jax.numpy as jnp
from jax import lax
from jax.experimental import pallas as pl
from jax.experimental.pallas import tpu as pltpu
from jax.sharding import PartitionSpec as P

TY = 2
GROUP = 8
MESH = pl.DeviceIdType.MESH

center_shift = 0.25
half_range = 1.0


def dot(a, b):
    return jnp.dot(a, b, precision=lax.Precision.HIGHEST, preferred_element_type=jnp.float32)


def kernel(
    rows, cols, tx,
    vec_hbm, blk_hbm, pattern, counts, out_hbm,
    vec, blk, amat, first, out, halo, relay, halo_col, col_relay,
    load_sem, store_sem, near_send, near_recv, far_send, far_recv, pass_send, pass_recv, col_send, col_recv,
    turn_send, turn_recv, near_ready, far_ready,
):
    bs = blk.shape[2]
    width = vec.shape[-1]
    slots = blk.shape[1]
    sites = TY * tx
    me_r, me_c = lax.axis_index("row"), lax.axis_index("col")
    even = 1 - lax.rem(me_r, 2)
    partner = (me_r - 1 + 2 * even, me_c)
    relay_to = (lax.rem(me_r + rows + 2 - 4 * even, rows), me_c)
    relay_from = (lax.rem(me_r + rows - 2 + 4 * even, rows), me_c)
    facing = (even, 1 - even)
    left, right = lax.rem(me_c + cols - 1, cols), lax.rem(me_c + 1, cols)
    place = lax.rem(me_c, GROUP)
    group = me_c - place
    group_before, group_after = lax.rem(group + cols - GROUP, cols), lax.rem(group + GROUP, cols)
    core = lax.rem(me_c, 2)
    inner = (place > 0) & (place < GROUP - 1)

    load_blk = pltpu.make_async_copy(blk_hbm, blk, load_sem.at[0])
    load_vec = pltpu.make_async_copy(vec_hbm, vec, load_sem.at[1])
    load_vec.start()
    load_blk.start()

    barrier = pltpu.get_barrier_semaphore()

    def tell(row, column):
        pl.semaphore_signal(barrier, inc=1, device_id=(row, column), device_id_type=MESH)

    def leader(column):
        return column - lax.rem(column, 2)

    tell(partner[0], leader(me_c))
    tell(me_r, leader(left))

    @pl.when(core == 1)
    def _():
        tell(me_r, leader(right))

    @pl.when(place == 0)
    def _():
        for k in range(3):
            tell(me_r, group_before + 2 * k)

    @pl.when(place == GROUP - 1)
    def _():
        for k in range(3):
            tell(me_r, group_after + 2 * k + 2)

    @pl.when(inner)
    def _():
        tell(me_r, group + (GROUP - 2) * core)

    tell(relay_from[0], leader(me_c) + 1)

    @pl.when(core == 0)
    def _():
        at_end = (place == 0) | (place == GROUP - 2)

        @pl.when(at_end)
        def _():
            pl.semaphore_wait(barrier, 9)

        @pl.when(jnp.logical_not(at_end))
        def _():
            pl.semaphore_wait(barrier, 7)

        pl.semaphore_signal(near_ready, inc=1, device_id=(me_r, me_c + 1), device_id_type=MESH)

    @pl.when(core == 1)
    def _():
        pl.semaphore_wait(near_ready, 1)

    def site(kind, v):
        return facing[kind] * tx + v

    def near_copy(source, step, v):
        return pltpu.make_async_remote_copy(
            src_ref=source.at[site(0, v)], dst_ref=halo.at[step, 0, v],
            send_sem=near_send.at[step, v], recv_sem=near_recv.at[step, v],
            device_id=partner, device_id_type=MESH,
        )

    def far_copy(source, step, v):
        return pltpu.make_async_remote_copy(
            src_ref=source.at[site(1, v)], dst_ref=relay.at[step, v],
            send_sem=far_send.at[step, v], recv_sem=far_recv.at[step, v],
            device_id=relay_to, device_id_type=MESH,
        )

    def pass_copy(step, v):
        return pltpu.make_async_remote_copy(
            src_ref=relay.at[step, v], dst_ref=halo.at[step, 1, v],
            send_sem=pass_send.at[step, v], recv_sem=pass_recv.at[step, v],
            device_id=partner, device_id_type=MESH,
        )

    def col_copy(source, step, side, u):
        v = 0 if side == 0 else tx - 1
        return pltpu.make_async_remote_copy(
            src_ref=source.at[u * tx + v], dst_ref=halo_col.at[step, 1 - side, u],
            send_sem=col_send.at[step, 1 - side, u], recv_sem=col_recv.at[step, 1 - side, u],
            device_id=(me_r, (left, right)[side]), device_id_type=MESH,
        )

    def quarter_copy(source, step, side, u, part):
        a = u * tx + (0 if side == 0 else tx - 1)
        k = 2 * u + part
        if k == 3:
            dst, recv, column = halo_col.at[step, 1 - side, u, part], col_recv.at[step, 1 - side, u], (left, right)[side]
        else:
            dst, recv, column = col_relay.at[step], turn_recv.at[step], group + 2 * k + 2 - side
        return pltpu.make_async_remote_copy(
            src_ref=source.at[a, part], dst_ref=dst,
            send_sem=col_send.at[step, 1 - side, u], recv_sem=recv,
            device_id=(me_r, column), device_id_type=MESH,
        )

    def turn_copy(step):
        k = (place - 1) // 2
        u, part = k // 2, lax.rem(k, 2)
        column = jnp.where(core == 1, group_after, group_before + GROUP - 1)
        return pltpu.make_async_remote_copy(
            src_ref=col_relay.at[step], dst_ref=halo_col.at[step, 1 - core, u, part],
            send_sem=turn_send.at[step], recv_sem=col_recv.at[step, 1 - core, u],
            device_id=(me_r, column), device_id_type=MESH,
        )

    def send_columns(source, step):
        for side in range(2):
            end = (GROUP - 1) * side

            @pl.when(place == end)
            def _():
                for u in range(TY):
                    for part in range(2):
                        quarter_copy(source, step, side, u, part).start()

            @pl.when(place != end)
            def _():
                for u in range(TY):
                    col_copy(source, step, side, u).start()

    def turn(step):
        @pl.when(inner)
        def _():
            pltpu.make_async_copy(col_relay.at[step], col_relay.at[step], turn_recv.at[step]).wait()
            turn_copy(step).start()

    edges = [0, tx - 1]
    inside = list(range(1, tx - 1))
    send_columns(vec_hbm, 0)
    for v in edges:
        near_copy(vec_hbm, 0, v).start()

    def site_id(y, x):
        return ((y // TY * cols + x // tx) * TY + y % TY) * tx + x % tx

    load_blk.wait()
    for u in range(TY):
        for v in range(tx):
            a = u * tx + v
            y, x = me_r * TY + u, me_c * tx + v
            up = lax.rem(y + TY * rows - 1, TY * rows)
            down = lax.rem(y + 1, TY * rows)
            west = lax.rem(x + tx * cols - 1, tx * cols)
            east = lax.rem(x + 1, tx * cols)
            target = [(y, x), (down if u == 0 else up, x), (y, west), (y, east), (up if u == 0 else down, x)]
            for d in range(5):
                name = site_id(*target[d])
                slot = jnp.int32(0)
                for s in range(1, slots):
                    slot = jnp.where(pattern[a, s] == name, s, slot)
                live = jnp.where(slot < counts[a], 1.0, 0.0)
                amat[a, :, d * bs:(d + 1) * bs] = blk[a, slot] * live

    turn(0)

    @pl.when(me_r < 2)
    def _():
        for v in inside:
            near_copy(vec_hbm, 0, v).start()

    @pl.when(core == 1)
    def _():
        pl.semaphore_wait(barrier, 2)
        pl.semaphore_signal(far_ready, inc=1, device_id=(me_r, me_c - 1), device_id_type=MESH)

    @pl.when(core == 0)
    def _():
        pl.semaphore_wait(far_ready, 1)

    for v in edges + inside:
        far_copy(vec_hbm, 0, v).start()
    for v in edges:
        far_copy(vec_hbm, 0, v).wait_recv()
        pass_copy(0, v).start()

    @pl.when(me_r >= 2)
    def _():
        for v in inside:
            near_copy(vec_hbm, 0, v).start()

    for v in inside:
        far_copy(vec_hbm, 0, v).wait_recv()
        pass_copy(0, v).start()
    load_vec.wait()

    def block(ref):
        return ref[...].reshape(bs, width)

    def store(ref, a, value):
        ref[a] = value.reshape(2, bs // 2, width)

    def coupled(a, first_d, *refs):
        field = jnp.concatenate([block(ref) for ref in refs], axis=0)
        return dot(amat[a, :, first_d * bs:(first_d + len(refs)) * bs], field)

    def partial(field, u, v):
        a = u * tx + v
        total = coupled(a, 0, field.at[a], field.at[(1 - u) * tx + v]) - center_shift * block(field.at[a])
        if v == 0:
            return total + coupled(a, 3, field.at[a + 1])
        if v == tx - 1:
            return total + coupled(a, 2, field.at[a - 1])
        return total + coupled(a, 2, field.at[a - 1], field.at[a + 1])

    def from_columns(step, u, v):
        side = 0 if v == 0 else 1
        return coupled(u * tx + v, 2 + side, halo_col.at[step, side, u])

    def from_rows(field, step, kind, v):
        if kind == 0:
            near_copy(field, step, v).wait_recv()
        else:
            pass_copy(step, v).wait_recv()
        return coupled(site(kind, v), 4, halo.at[step, kind, v])

    def wait_columns(field, step):
        for u in range(TY):
            for side in range(2):
                col_copy(field, step, side, u).wait_recv()

    for v in inside + edges:
        for u in range(TY):
            store(first, u * tx + v, partial(vec, u, v))
    wait_columns(vec, 0)
    for v in edges:
        for u in range(TY):
            a = u * tx + v
            store(first, a, block(first.at[a]) + from_columns(0, u, v))
    for some in (edges, inside):
        for kind in range(2):
            for v in some:
                a = site(kind, v)
                store(first, a, (block(first.at[a]) + from_rows(vec, 0, kind, v)) / half_range)
                if kind == 0:
                    near_copy(first, 1, v).start()
                else:
                    far_copy(first, 1, v).start()
        if some is edges:
            send_columns(first, 1)
        for v in some:
            far_copy(first, 1, v).wait_recv()
            pass_copy(1, v).start()
        if some is edges:
            turn(1)

    def finish(a, value):
        store(out, a, 2.0 * (value / half_range) - block(vec.at[a]))
        pltpu.make_async_copy(out.at[a], out_hbm.at[a], store_sem.at[a]).start()

    for v in inside + edges:
        for u in range(TY):
            store(out, u * tx + v, partial(first, u, v))
    for kind in range(2):
        for v in edges:
            a = site(kind, v)
            store(out, a, block(out.at[a]) + from_rows(first, 1, kind, v))
    for v in inside:
        a = site(0, v)
        finish(a, block(out.at[a]) + from_rows(first, 1, 0, v))
    wait_columns(first, 1)
    for v in edges:
        for u in range(TY):
            a = u * tx + v
            finish(a, block(out.at[a]) + from_columns(1, u, v))
    for v in inside:
        a = site(1, v)
        finish(a, block(out.at[a]) + from_rows(first, 1, 1, v))

    for step, field in ((0, vec_hbm), (1, first)):
        for v in range(tx):
            near_copy(field, step, v).wait_send()
            far_copy(field, step, v).wait_send()
            pass_copy(step, v).wait_send()
        for u in range(TY):
            for side in range(2):
                col_copy(field, step, side, u).wait_send()

        @pl.when(inner)
        def _():
            turn_copy(step).wait_send()

    for a in range(sites):
        pltpu.make_async_copy(out.at[a], out_hbm.at[a], store_sem.at[a]).wait()


def body(vectors, blocks, pattern, counts):
    local, slots, bs, _ = blocks.shape
    width = vectors.shape[1]
    rows, cols = lax.axis_size("row"), lax.axis_size("col")
    tx = local // TY
    f32 = jnp.float32
    anywhere = pl.BlockSpec(memory_space=pl.ANY)
    scalars = pl.BlockSpec(memory_space=pltpu.SMEM)
    dma = pltpu.SemaphoreType.DMA
    result = pl.pallas_call(
        functools.partial(kernel, rows, cols, tx),
        out_shape=jax.ShapeDtypeStruct((local, 2, bs // 2, width), f32),
        in_specs=[anywhere, anywhere, scalars, scalars],
        out_specs=anywhere,
        scratch_shapes=[
            pltpu.VMEM((local, 2, bs // 2, width), f32),
            pltpu.VMEM((local, slots, bs, bs), f32),
            pltpu.VMEM((local, bs, slots * bs), f32),
            pltpu.VMEM((local, 2, bs // 2, width), f32),
            pltpu.VMEM((local, 2, bs // 2, width), f32),
            pltpu.VMEM((2, 2, tx, 2, bs // 2, width), f32),
            pltpu.VMEM((2, tx, 2, bs // 2, width), f32),
            pltpu.VMEM((2, 2, TY, 2, bs // 2, width), f32),
            pltpu.VMEM((2, bs // 2, width), f32),
            dma((2,)),
            dma((local,)),
            dma((2, tx)),
            dma((2, tx)),
            dma((2, tx)),
            dma((2, tx)),
            dma((2, tx)),
            dma((2, tx)),
            dma((2, 2, TY)),
            dma((2, 2, TY)),
            dma((2,)),
            dma((2,)),
            pltpu.SemaphoreType.REGULAR,
            pltpu.SemaphoreType.REGULAR,
        ],
        compiler_params=pltpu.CompilerParams(
            collective_id=0, has_side_effects=True, vmem_limit_bytes=60 << 20
        ),
        cost_estimate=pl.CostEstimate(
            flops=2 * 2 * local * slots * bs * bs * width, bytes_accessed=5 << 20, transcendentals=0
        ),
        name="filter_steps",
    )(vectors.reshape(local, 2, bs // 2, width), blocks, pattern, counts)
    return result.reshape(local * bs, width)


def solution(mesh):
    placed = (
        P(("row", "col"), None),
        P(("row", "col"), None, None, None),
        P(("row", "col"), None),
        P(("row", "col")),
    )
    return jax.shard_map(
        body, mesh=mesh, in_specs=placed, out_specs=P(("row", "col"), None), check_vma=False
    )
```

time: 121 us -> 112 us (0.926)
  the two profiles are of different devices: /device:TPU:576 before, /device:TPU:8 now
where the time goes in v2:
time: 112 us
  Pallas kernels  110 us (98%)
  local copies, waits for them, and re-layouts  2.26 us (2%)
    pallas_call x1, Pallas kernels, body(): pl.pallas_call(functools.partial(kernel, rows, cols, tx), out_shape=jax.S...  110 us
    unnamed x1, local copies, waits for them, and re-layouts  2.26 us

profile of v2, /device:TPU:8, one launch (start us, length us, event | category | flops | bytes accessed | tf_op | source)
XLA Modules:
  0.0 111.9 jit_solution(17029448696238181871)
XLA Ops:
  0.0 109.6 %filter_steps.1 = f32[8,2,64,256]{3,2,1,0:T(8,128)} custom-call(f32[8,2,64,256]{3,2,1,0:T(8,128)} %bitcast.3, f32[8,5,128,128]{3,2,1,0:T(8,128)} %blk_hbm.1, s32[8,5]{1,0:T(8,128)} %pattern.1, s32[8]{0:T(128)} %counts.1), custom_call_target="tpu_custom_call" | custom-call | flops 671088640 | bytes 5242880 | tf_op jit(solution)/shard_map/filter_steps/pallas_call | solution.py:344
  109.6 2.3 %copy.6 = f32[1024,256]{1,0:T(8,128)} copy(f32[1024,256]{1,0:T(8,128)} %bitcast.2) | data formatting | bytes 2097152

commit v3 on v2

--- a/solution.py
+++ b/solution.py
@@ -21,15 +21,14 @@
 
 def kernel(
     rows, cols, tx,
-    vec_hbm, blk_hbm, pattern, counts, out_hbm,
-    vec, blk, amat, first, out, halo, relay, halo_col, col_relay,
-    load_sem, store_sem, near_send, near_recv, far_send, far_recv, pass_send, pass_recv, col_send, col_recv,
+    vec_hbm, blk_hbm, pattern_hbm, counts_hbm, out,
+    pattern, counts, vec, blk, amat, first, halo, relay, halo_col, col_relay,
+    load_sem, near_send, near_recv, far_send, far_recv, pass_send, pass_recv, col_send, col_recv,
     turn_send, turn_recv, near_ready, far_ready,
 ):
     bs = blk.shape[2]
     width = vec.shape[-1]
     slots = blk.shape[1]
-    sites = TY * tx
     me_r, me_c = lax.axis_index("row"), lax.axis_index("col")
     even = 1 - lax.rem(me_r, 2)
     partner = (me_r - 1 + 2 * even, me_c)
@@ -45,52 +44,52 @@
 
     load_blk = pltpu.make_async_copy(blk_hbm, blk, load_sem.at[0])
     load_vec = pltpu.make_async_copy(vec_hbm, vec, load_sem.at[1])
+    load_pattern = pltpu.make_async_copy(pattern_hbm, pattern, load_sem.at[2])
+    load_counts = pltpu.make_async_copy(counts_hbm, counts, load_sem.at[3])
+
+    barrier = pltpu.get_barrier_semaphore()
+
+    def tell(row, column):
+        pl.semaphore_signal(barrier, inc=1, device_id=(row, column), device_id_type=MESH)
+
+    def leader(column):
+        return column - lax.rem(column, 2)
+
+    tell(partner[0], leader(me_c))
+
+    @pl.when(core == 1)
+    def _():
+        tell(me_r, me_c - 1)
+
+    @pl.when(core == 0)
+    def _():
+        tell(me_r, left)
+
+    tell(me_r, leader(right) + 1)
+    tell(relay_from[0], leader(me_c) + 1)
+
+    @pl.when(place == 0)
+    def _():
+        for k in range(3):
+            tell(me_r, group_before + 2 * k + 1)
+
+    @pl.when(place == GROUP - 1)
+    def _():
+        for k in range(3):
+            tell(me_r, group_after + 2 * k + 3)
+
+    @pl.when(inner)
+    def _():
+        tell(me_r, group + 1 + (GROUP - 2) * core)
+
+    load_pattern.start()
+    load_counts.start()
     load_vec.start()
     load_blk.start()
 
-    barrier = pltpu.get_barrier_semaphore()
-
-    def tell(row, column):
-        pl.semaphore_signal(barrier, inc=1, device_id=(row, column), device_id_type=MESH)
-
-    def leader(column):
-        return column - lax.rem(column, 2)
-
-    tell(partner[0], leader(me_c))
-    tell(me_r, leader(left))
-
-    @pl.when(core == 1)
-    def _():
-        tell(me_r, leader(right))
-
-    @pl.when(place == 0)
-    def _():
-        for k in range(3):
-            tell(me_r, group_before + 2 * k)
-
-    @pl.when(place == GROUP - 1)
-    def _():
-        for k in range(3):
-            tell(me_r, group_after + 2 * k + 2)
-
-    @pl.when(inner)
-    def _():
-        tell(me_r, group + (GROUP - 2) * core)
-
-    tell(relay_from[0], leader(me_c) + 1)
-
     @pl.when(core == 0)
     def _():
-        at_end = (place == 0) | (place == GROUP - 2)
-
-        @pl.when(at_end)
-        def _():
-            pl.semaphore_wait(barrier, 9)
-
-        @pl.when(jnp.logical_not(at_end))
-        def _():
-            pl.semaphore_wait(barrier, 7)
-
+        pl.semaphore_wait(barrier, 3)
         pl.semaphore_signal(near_ready, inc=1, device_id=(me_r, me_c + 1), device_id_type=MESH)
 
     @pl.when(core == 1)
@@ -175,13 +174,41 @@
 
     edges = [0, tx - 1]
     inside = list(range(1, tx - 1))
+    for v in edges:
+        near_copy(vec_hbm, 0, v).start()
+
+    @pl.when(me_r < 2)
+    def _():
+        for v in inside:
+            near_copy(vec_hbm, 0, v).start()
+
+    at_end = (place == 1) | (place == GROUP - 1)
+
+    @pl.when((core == 1) & at_end)
+    def _():
+        pl.semaphore_wait(barrier, 9)
+
+    @pl.when((core == 1) & jnp.logical_not(at_end))
+    def _():
+        pl.semaphore_wait(barrier, 7)
+
+    @pl.when(core == 1)
+    def _():
+        pl.semaphore_signal(far_ready, inc=1, device_id=(me_r, me_c - 1), device_id_type=MESH)
+
+    @pl.when(core == 0)
+    def _():
+        pl.semaphore_wait(far_ready, 1)
+
     send_columns(vec_hbm, 0)
-    for v in edges:
-        near_copy(vec_hbm, 0, v).start()
+    for v in edges + inside:
+        far_copy(vec_hbm, 0, v).start()
 
     def site_id(y, x):
         return ((y // TY * cols + x // tx) * TY + y % TY) * tx + x % tx
 
+    load_pattern.wait()
+    load_counts.wait()
     load_blk.wait()
     for u in range(TY):
         for v in range(tx):
@@ -201,23 +228,6 @@
                 amat[a, :, d * bs:(d + 1) * bs] = blk[a, slot] * live
 
     turn(0)
-
-    @pl.when(me_r < 2)
-    def _():
-        for v in inside:
-            near_copy(vec_hbm, 0, v).start()
-
-    @pl.when(core == 1)
-    def _():
-        pl.semaphore_wait(barrier, 2)
-        pl.semaphore_signal(far_ready, inc=1, device_id=(me_r, me_c - 1), device_id_type=MESH)
-
-    @pl.when(core == 0)
-    def _():
-        pl.semaphore_wait(far_ready, 1)
-
-    for v in edges + inside:
-        far_copy(vec_hbm, 0, v).start()
     for v in edges:
         far_copy(vec_hbm, 0, v).wait_recv()
         pass_copy(0, v).start()
@@ -275,37 +285,45 @@
         for u in range(TY):
             a = u * tx + v
             store(first, a, block(first.at[a]) + from_columns(0, u, v))
-    for some in (edges, inside):
-        for kind in range(2):
-            for v in some:
-                a = site(kind, v)
-                store(first, a, (block(first.at[a]) + from_rows(vec, 0, kind, v)) / half_range)
-                if kind == 0:
-                    near_copy(first, 1, v).start()
-                else:
-                    far_copy(first, 1, v).start()
-        if some is edges:
-            send_columns(first, 1)
+
+    def first_step(kind, some):
+        for v in some:
+            a = site(kind, v)
+            store(first, a, (block(first.at[a]) + from_rows(vec, 0, kind, v)) / half_range)
+            if kind == 0:
+                near_copy(first, 1, v).start()
+            else:
+                far_copy(first, 1, v).start()
+
+    def pass_on(some):
         for v in some:
             far_copy(first, 1, v).wait_recv()
             pass_copy(1, v).start()
-        if some is edges:
-            turn(1)
+
+    first_step(0, edges)
+    first_step(1, edges)
+    send_columns(first, 1)
+    first_step(0, inside)
+    pass_on(edges)
+    turn(1)
+    first_step(1, inside)
+    pass_on(inside)
 
     def finish(a, value):
         store(out, a, 2.0 * (value / half_range) - block(vec.at[a]))
-        pltpu.make_async_copy(out.at[a], out_hbm.at[a], store_sem.at[a]).start()
 
     for v in inside + edges:
         for u in range(TY):
             store(out, u * tx + v, partial(first, u, v))
-    for kind in range(2):
-        for v in edges:
-            a = site(kind, v)
-            store(out, a, block(out.at[a]) + from_rows(first, 1, kind, v))
+    for v in edges:
+        a = site(0, v)
+        store(out, a, block(out.at[a]) + from_rows(first, 1, 0, v))
     for v in inside:
         a = site(0, v)
         finish(a, block(out.at[a]) + from_rows(first, 1, 0, v))
+    for v in edges:
+        a = site(1, v)
+        store(out, a, block(out.at[a]) + from_rows(first, 1, 1, v))
     wait_columns(first, 1)
     for v in edges:
         for u in range(TY):
@@ -327,9 +345,6 @@
         @pl.when(inner)
         def _():
             turn_copy(step).wait_send()
-
-    for a in range(sites):
-        pltpu.make_async_copy(out.at[a], out_hbm.at[a], store_sem.at[a]).wait()
 
 
 def body(vectors, blocks, pattern, counts):
@@ -338,26 +353,29 @@
     rows, cols = lax.axis_size("row"), lax.axis_size("col")
     tx = local // TY
     f32 = jnp.float32
-    anywhere = pl.BlockSpec(memory_space=pl.ANY)
-    scalars = pl.BlockSpec(memory_space=pltpu.SMEM)
+    stays = pl.BlockSpec(memory_space=pltpu.HBM)
+    operands = [
+        pltpu.with_memory_space_constraint(operand, pltpu.HBM)
+        for operand in (vectors.reshape(local, 2, bs // 2, width), blocks, pattern, counts)
+    ]
     dma = pltpu.SemaphoreType.DMA
     result = pl.pallas_call(
         functools.partial(kernel, rows, cols, tx),
         out_shape=jax.ShapeDtypeStruct((local, 2, bs // 2, width), f32),
-        in_specs=[anywhere, anywhere, scalars, scalars],
-        out_specs=anywhere,
+        in_specs=[stays] * 4,
+        out_specs=pl.BlockSpec(memory_space=pltpu.VMEM),
         scratch_shapes=[
+            pltpu.SMEM(pattern.shape, jnp.int32),
+            pltpu.SMEM(counts.shape, jnp.int32),
             pltpu.VMEM((local, 2, bs // 2, width), f32),
             pltpu.VMEM((local, slots, bs, bs), f32),
             pltpu.VMEM((local, bs, slots * bs), f32),
-            pltpu.VMEM((local, 2, bs // 2, width), f32),
             pltpu.VMEM((local, 2, bs // 2, width), f32),
             pltpu.VMEM((2, 2, tx, 2, bs // 2, width), f32),
             pltpu.VMEM((2, tx, 2, bs // 2, width), f32),
             pltpu.VMEM((2, 2, TY, 2, bs // 2, width), f32),
             pltpu.VMEM((2, bs // 2, width), f32),
-            dma((2,)),
-            dma((local,)),
+            dma((4,)),
             dma((2, tx)),
             dma((2, tx)),
             dma((2, tx)),
@@ -372,13 +390,13 @@
             pltpu.SemaphoreType.REGULAR,
         ],
         compiler_params=pltpu.CompilerParams(
-            collective_id=0, has_side_effects=True, vmem_limit_bytes=60 << 20
+            collective_id=0, has_side_effects=True, vmem_limit_bytes=24 << 20
         ),
         cost_estimate=pl.CostEstimate(
             flops=2 * 2 * local * slots * bs * bs * width, bytes_accessed=5 << 20, transcendentals=0
         ),
         name="filter_steps",
-    )(vectors.reshape(local, 2, bs // 2, width), blocks, pattern, counts)
+    )(*operands)
     return result.reshape(local * bs, width)
 
 

time: 112 us -> 108 us (0.964)
  the two profiles are of different devices: /device:TPU:8 before, /device:TPU:16 now
where the time goes in v3:
time: 108 us
  Pallas kernels  107 us (99%)
    pallas_call x1, Pallas kernels, body(): pl.pallas_call(functools.partial(kernel, rows, cols, tx), out_shape=jax.S...  107 us

profile of v3, /device:TPU:16, one launch (start us, length us, event | category | flops | bytes accessed | tf_op | source)
XLA Modules:
  0.0 107.8 jit_solution(12337612268222390877)
XLA Ops:
  0.0 106.8 %filter_steps.1 = f32[8,2,64,256]{3,2,1,0:T(8,128)S(1)} custom-call(f32[8,2,64,256]{3,2,1,0:T(8,128)} %bitcast.3, f32[8,5,128,128]{3,2,1,0:T(8,128)} %blk_hbm.1, s32[8,5]{1,0:T(8,128)} %pattern_hbm.1, s32[8]{0:T(128)} %counts_hbm.1), custom_call_target="tpu_custom_call" | custom-call | flops 671088640 | bytes 5242880 | tf_op jit(solution)/shard_map/filter_steps/pallas_call | solution.py:362
  106.8 1.0 copy.6

commit v4 on v3

--- a/solution.py
+++ b/solution.py
@@ -24,7 +24,7 @@
     vec_hbm, blk_hbm, pattern_hbm, counts_hbm, out,
     pattern, counts, vec, blk, amat, first, halo, relay, halo_col, col_relay,
     load_sem, near_send, near_recv, far_send, far_recv, pass_send, pass_recv, col_send, col_recv,
-    turn_send, turn_recv, near_ready, far_ready,
+    turn_send, turn_recv, rest_ready,
 ):
     bs = blk.shape[2]
     width = vec.shape[-1]
@@ -55,46 +55,32 @@
     def leader(column):
         return column - lax.rem(column, 2)
 
-    tell(partner[0], leader(me_c))
+    tell(*partner)
+    tell(me_r, leader(left))
+    tell(relay_from[0], leader(me_c))
 
     @pl.when(core == 1)
     def _():
-        tell(me_r, me_c - 1)
-
-    @pl.when(core == 0)
-    def _():
-        tell(me_r, left)
-
-    tell(me_r, leader(right) + 1)
-    tell(relay_from[0], leader(me_c) + 1)
+        tell(me_r, right)
 
     @pl.when(place == 0)
     def _():
         for k in range(3):
-            tell(me_r, group_before + 2 * k + 1)
+            tell(me_r, group_before + 2 * k)
 
     @pl.when(place == GROUP - 1)
     def _():
         for k in range(3):
-            tell(me_r, group_after + 2 * k + 3)
+            tell(me_r, group_after + 2 * k + 2)
 
     @pl.when(inner)
     def _():
-        tell(me_r, group + 1 + (GROUP - 2) * core)
+        tell(me_r, group + (GROUP - 2) * core)
 
     load_pattern.start()
     load_counts.start()
     load_vec.start()
     load_blk.start()
-
-    @pl.when(core == 0)
-    def _():
-        pl.semaphore_wait(barrier, 3)
-        pl.semaphore_signal(near_ready, inc=1, device_id=(me_r, me_c + 1), device_id_type=MESH)
-
-    @pl.when(core == 1)
-    def _():
-        pl.semaphore_wait(near_ready, 1)
 
     def site(kind, v):
         return facing[kind] * tx + v
@@ -174,31 +160,43 @@
 
     edges = [0, tx - 1]
     inside = list(range(1, tx - 1))
-    for v in edges:
-        near_copy(vec_hbm, 0, v).start()
-
-    @pl.when(me_r < 2)
-    def _():
-        for v in inside:
+    def forward():
+        for v in edges + inside:
+            far_copy(vec_hbm, 0, v).wait_recv()
+            pass_copy(0, v).start()
+
+    def start_near():
+        for v in edges + inside:
             near_copy(vec_hbm, 0, v).start()
 
-    at_end = (place == 1) | (place == GROUP - 1)
-
-    @pl.when((core == 1) & at_end)
-    def _():
-        pl.semaphore_wait(barrier, 9)
-
-    @pl.when((core == 1) & jnp.logical_not(at_end))
-    def _():
-        pl.semaphore_wait(barrier, 7)
+    early = (me_r == 0) & (core == 1)
+    at_end = (place == 0) | (place == GROUP - 2)
+
+    @pl.when((core == 0) & at_end)
+    def _():
+        pl.semaphore_wait(barrier, 10)
+
+    @pl.when((core == 0) & jnp.logical_not(at_end))
+    def _():
+        pl.semaphore_wait(barrier, 8)
+
+    @pl.when(core == 0)
+    def _():
+        pl.semaphore_signal(rest_ready, inc=1, device_id=(me_r, me_c + 1), device_id_type=MESH)
+        start_near()
 
     @pl.when(core == 1)
     def _():
-        pl.semaphore_signal(far_ready, inc=1, device_id=(me_r, me_c - 1), device_id_type=MESH)
-
-    @pl.when(core == 0)
-    def _():
-        pl.semaphore_wait(far_ready, 1)
+        pl.semaphore_wait(barrier, 1)
+        start_near()
+
+    @pl.when(early)
+    def _():
+        forward()
+
+    @pl.when(core == 1)
+    def _():
+        pl.semaphore_wait(rest_ready, 1)
 
     send_columns(vec_hbm, 0)
     for v in edges + inside:
@@ -228,18 +226,11 @@
                 amat[a, :, d * bs:(d + 1) * bs] = blk[a, slot] * live
 
     turn(0)
-    for v in edges:
-        far_copy(vec_hbm, 0, v).wait_recv()
-        pass_copy(0, v).start()
-
-    @pl.when(me_r >= 2)
-    def _():
-        for v in inside:
-            near_copy(vec_hbm, 0, v).start()
-
-    for v in inside:
-        far_copy(vec_hbm, 0, v).wait_recv()
-        pass_copy(0, v).start()
+
+    @pl.when(jnp.logical_not(early))
+    def _():
+        forward()
+
     load_vec.wait()
 
     def block(ref):
@@ -304,8 +295,8 @@
     first_step(1, edges)
     send_columns(first, 1)
     first_step(0, inside)
+    turn(1)
     pass_on(edges)
-    turn(1)
     first_step(1, inside)
     pass_on(inside)
 
@@ -387,7 +378,6 @@
             dma((2,)),
             dma((2,)),
             pltpu.SemaphoreType.REGULAR,
-            pltpu.SemaphoreType.REGULAR,
         ],
         compiler_params=pltpu.CompilerParams(
             collective_id=0, has_side_effects=True, vmem_limit_bytes=24 << 20

time: 108 us -> 106 us (0.981)
  Pallas kernels: 107 us -> 105 us
    pallas_call x1, Pallas kernels: 107 us -> 105 us  [body(): pl.pallas_call(functools.partial(kernel, rows, cols, tx), out_shape=jax.S...]
where the time goes in v4:
time: 106 us
  Pallas kernels  105 us (99%)
    pallas_call x1, Pallas kernels, body(): pl.pallas_call(functools.partial(kernel, rows, cols, tx), out_shape=jax.S...  105 us

profile of v4, /device:TPU:16, one launch (start us, length us, event | category | flops | bytes accessed | tf_op | source)
XLA Modules:
  0.0 105.7 jit_solution(5945886035792902595)
XLA Ops:
  0.0 104.7 %filter_steps.1 = f32[8,2,64,256]{3,2,1,0:T(8,128)S(1)} custom-call(f32[8,2,64,256]{3,2,1,0:T(8,128)} %bitcast.3, f32[8,5,128,128]{3,2,1,0:T(8,128)} %blk_hbm.1, s32[8,5]{1,0:T(8,128)} %pattern_hbm.1, s32[8]{0:T(128)} %counts_hbm.1), custom_call_target="tpu_custom_call" | custom-call | flops 671088640 | bytes 5242880 | tf_op jit(solution)/shard_map/filter_steps/pallas_call | solution.py:353
  104.7 1.0 copy.6

commit v5 on v4

--- a/solution.py
+++ b/solution.py
@@ -162,12 +162,14 @@
     inside = list(range(1, tx - 1))
     def forward():
         for v in edges + inside:
-            far_copy(vec_hbm, 0, v).wait_recv()
+            far_copy(vec, 0, v).wait_recv()
             pass_copy(0, v).start()
 
     def start_near():
         for v in edges + inside:
-            near_copy(vec_hbm, 0, v).start()
+            near_copy(vec, 0, v).start()
+
+    load_vec.wait()
 
     early = (me_r == 0) & (core == 1)
     at_end = (place == 0) | (place == GROUP - 2)
@@ -198,9 +200,9 @@
     def _():
         pl.semaphore_wait(rest_ready, 1)
 
-    send_columns(vec_hbm, 0)
+    send_columns(vec, 0)
     for v in edges + inside:
-        far_copy(vec_hbm, 0, v).start()
+        far_copy(vec, 0, v).start()
 
     def site_id(y, x):
         return ((y // TY * cols + x // tx) * TY + y % TY) * tx + x % tx
@@ -231,7 +233,6 @@
     def _():
         forward()
 
-    load_vec.wait()
 
     def block(ref):
         return ref[...].reshape(bs, width)

time: 106 us -> 104 us (0.981)
  the two profiles are of different devices: /device:TPU:16 before, /device:TPU:706 now
where the time goes in v5:
time: 104 us; the launch traced here: 103 us
  Pallas kernels  102 us (98%)
    pallas_call x1, Pallas kernels, body(): pl.pallas_call(functools.partial(kernel, rows, cols, tx), out_shape=jax.S...  102 us

profile of v5, /device:TPU:706, one launch (start us, length us, event | category | flops | bytes accessed | tf_op | source)
XLA Modules:
  0.0 103.5 jit_solution(11146850591095887059)
XLA Ops:
  0.0 102.5 %filter_steps.1 = f32[8,2,64,256]{3,2,1,0:T(8,128)S(1)} custom-call(f32[8,2,64,256]{3,2,1,0:T(8,128)} %bitcast.3, f32[8,5,128,128]{3,2,1,0:T(8,128)} %blk_hbm.1, s32[8,5]{1,0:T(8,128)} %pattern_hbm.1, s32[8]{0:T(128)} %counts_hbm.1), custom_call_target="tpu_custom_call" | custom-call | flops 671088640 | bytes 5242880 | tf_op jit(solution)/shard_map/filter_steps/pallas_call | solution.py:354
  102.5 1.0 copy.6
